TPU v7x, 32 devices: a whole 2x2x4 slice. The times are simulated.
32 devices in a mesh: band: 8 (over z, x), wgrp: 4 (over y, core).
Axes of the slice: x: 2, y: 2, z: 4, core: 2. Of those that a mesh axis runs over, the one named last changes fastest.
Arguments:
- visibilities: bfloat16 [4, 512, 512], P('wgrp', 'band'), may hold values from -6 to 6
- coordinates: bfloat16 [4, 512, 512], P('wgrp', 'band'), may hold values from -16 to 16
- block_index: int32 [4, 512], P('wgrp', 'band'), may hold values from 0 to 63
- counts: int32 [4, 64], P('wgrp', 'band'), may hold values from 1 to 8, as said below
- col_offset: int32 [4, 512], P('wgrp', 'band'), may hold values from 0 to 8160
Outputs:
- image_rows: float32 [4, 2, 256, 8192], P('wgrp', None, 'band')
Inputs may be any that keep to these rules, and one draw needn't show every extreme that they name: Entry d of a device's row counts the live slots of its list for band d; every device's entry for band 8 // 2 is exactly 8. `block_index`: slots past a list's count read a block too; their subgrids are zero. `col_offset`: A subgrid lies inside its band's rows and the grid's columns.
All inputs are finite; a program needn't handle non-finite values.
Results may differ from a plain program's by a relative error of at most 0.0036.
Values may be sent and summed in bfloat16 or wider, within the bound.
No kernel may reach another device: no remote copies, remote signals or barrier semaphores. Data moves between devices by JAX's collectives and lax.ppermute only.
A program may use at most 128 MiB of HBM per device.

v0:
```python
import functools
import math

import jax
import jax.numpy as jnp
import numpy as np
from jax import lax
from jax.experimental import pallas as pl
from jax.experimental.pallas import tpu as pltpu
from jax.sharding import PartitionSpec as P

S = 32
G = 8192
K = 256
CAP = 8
HALF = S // 2
N1 = 128
N2 = 64
DATA = 4 * K
ROW = DATA + 128
LO = 64
PI = math.pi

SIN_TERMS = (1.0, -1 / 6, 1 / 120, -1 / 5040, 1 / 362880, -1 / 39916800)
COS_TERMS = (1.0, -1 / 2, 1 / 24, -1 / 720, 1 / 40320, -1 / 3628800, 1 / 479001600)


def transform_tables():
    n1, n2 = np.arange(N1), np.arange(N2)
    outer = np.exp(-2j * np.pi * (np.outer(n1, n1) % N1) / N1)
    inner = np.exp(-2j * np.pi * (np.outer(n2, n2) % N2) / N2)
    twist = np.exp(-2j * np.pi * np.outer(n1, n2) / G) / math.sqrt(G * K)
    pair = np.kron(np.eye(2), inner)

    def real_form(m):
        return np.block([[m.real, -m.imag], [m.imag, m.real]])

    twist = np.concatenate([twist, twist], axis=1)
    return (
        jnp.asarray(real_form(outer), jnp.bfloat16),
        jnp.asarray(real_form(pair), jnp.bfloat16),
        jnp.asarray(np.stack([twist.real, twist.imag]), jnp.float32),
    )


def dot_last(left, right):
    return lax.dot_general(
        left, right, (((1,), (1,)), ((), ())), preferred_element_type=jnp.float32
    )


def dot_first(left, right):
    return lax.dot_general(
        left, right, (((0,), (0,)), ((), ())), preferred_element_type=jnp.float32
    )


def own_base(band_count, group_count):
    low = lax.axis_index("wgrp") < group_count // 2
    return jnp.where(low, 0, band_count), jnp.where(low, band_count, 0)


def pack_kernel(band_count, group_count, vis_ref, coord_ref, block_ref, count_ref, offset_ref, out_ref):
    own, mirror = own_base(band_count, group_count)
    slots = block_ref.shape[1]
    blocks = vis_ref.shape[0]
    lane = lax.broadcasted_iota(jnp.int32, (1, slots), 1)
    list_of = lane // CAP
    within = lane % CAP
    band_row = lax.broadcasted_iota(jnp.int32, (band_count, slots), 0)
    in_list = (band_row == list_of).astype(jnp.float32)
    counts = jnp.broadcast_to(count_ref[...].astype(jnp.float32), (8, band_count))
    live_count = jnp.dot(counts, in_list, preferred_element_type=jnp.float32)[0:1]
    live = (within.astype(jnp.float32) < live_count).astype(jnp.float32)
    chosen = (
        lax.broadcasted_iota(jnp.int32, (blocks, slots), 0) == block_ref[...]
    ).astype(jnp.float32)
    vis = dot_first((chosen * live).astype(jnp.bfloat16), vis_ref[...])
    coord = dot_first(chosen.astype(jnp.bfloat16), coord_ref[...])
    offsets = offset_ref[...]
    here = lax.broadcasted_iota(jnp.int32, (CAP, slots), 0) == within
    high = jnp.where(here, (offsets >> 7).astype(jnp.float32), 0.0).astype(jnp.bfloat16)
    low = jnp.where(here, (offsets & 127).astype(jnp.float32), 0.0).astype(jnp.bfloat16)
    slot_row = lax.broadcasted_iota(jnp.int32, (slots, 128), 0) // CAP
    column = lax.broadcasted_iota(jnp.int32, (slots, 128), 1)
    to_high = (slot_row == column).astype(jnp.bfloat16)
    to_low = (slot_row + LO == column).astype(jnp.bfloat16)
    meta = jnp.dot(high, to_high, preferred_element_type=jnp.float32) + jnp.dot(
        low, to_low, preferred_element_type=jnp.float32
    )
    for d in range(band_count):
        rows = slice(d * CAP, (d + 1) * CAP)
        message = jnp.concatenate([vis[rows], coord[rows], meta], axis=1).astype(jnp.bfloat16)
        out_ref[own + d] = message
        out_ref[mirror + band_count - 1 - d] = message


def square(z):
    re, im = z
    return re * re - im * im, 2.0 * (re * im)


def times(z, w):
    return z[0] * w[0] - z[1] * w[1], z[0] * w[1] + z[1] * w[0]


def unit_phasor(cycles):
    half = (cycles - jnp.round(cycles)) * PI
    x = half * half
    sine = jnp.full_like(x, SIN_TERMS[-1])
    for term in SIN_TERMS[-2::-1]:
        sine = sine * x + term
    cosine = jnp.full_like(x, COS_TERMS[-1])
    for term in COS_TERMS[-2::-1]:
        cosine = cosine * x + term
    sine = sine * half
    return 1.0 - 2.0 * (sine * sine), 2.0 * (sine * cosine)


def grid_kernel(
    band_count,
    group_count,
    recv_ref,
    outer_ref,
    inner_ref,
    twist_ref,
    out_ref,
    offset_vmem,
    offset_smem,
    tab_re,
    tab_im,
    eight_re,
    eight_im,
    grid_ref,
    rows_ref,
    offset_sem,
    out_sem,
):
    own, mirror = own_base(band_count, group_count)
    band = lax.axis_index("band")
    peers = 2 * band_count

    meta = recv_ref[:, :, DATA:].astype(jnp.float32).reshape(peers * CAP, 128)
    pick_row = lax.broadcasted_iota(jnp.int32, (8, 128), 0)
    pick_col = lax.broadcasted_iota(jnp.int32, (8, 128), 1)
    flipped = band_count - 1 - band
    wanted = jnp.where(
        pick_row == 0,
        band,
        jnp.where(pick_row == 1, band + LO, jnp.where(pick_row == 2, flipped, flipped + LO)),
    )
    pick = (pick_col == wanted).astype(jnp.bfloat16)
    picked = dot_last(pick, meta.astype(jnp.bfloat16))
    offset_vmem[0:1] = (picked[0:1] * 128.0 + picked[1:2]).astype(jnp.int32)
    offset_vmem[1:2] = (G - S) - (picked[2:3] * 128.0 + picked[3:4]).astype(jnp.int32)
    to_smem = pltpu.make_async_copy(offset_vmem, offset_smem, offset_sem)
    to_smem.start()

    def clear(step, _):
        grid_ref[pl.ds(pl.multiple_of(step * 2 * S, 2 * S), 2 * S), :] = jnp.zeros(
            (2 * S, 128), jnp.float32
        )
        return 0

    lax.fori_loop(0, (N1 + 2) // 2, clear, 0)
    to_smem.wait()

    lane = lax.broadcasted_iota(jnp.int32, (HALF, 128), 1)
    first_half = lane < N2
    lane_in = lane & (N2 - 1)
    empty = jnp.zeros((S, 2 * K), jnp.bfloat16)
    chunks = 2 * K // 128

    def one_list(peer, mirrored):
        block = recv_ref[peer].astype(jnp.float32)
        vis = (block[:, 0:K], block[:, K : 2 * K])
        e1 = unit_phasor(block[:, 2 * K : 4 * K] * (1.0 / S))
        e2 = square(e1)
        e3 = times(e2, e1)
        e4 = square(e2)
        one = (jnp.ones_like(e1[0]), jnp.zeros_like(e1[0]))
        steps = (one, e1, e2, e3, e4, times(e4, e1), square(e3), times(e4, e3))
        e8 = square(e4)
        for b, e in enumerate(steps):
            place = CAP - 1 - b if mirrored else b
            weighted = vis if b == 0 else times(vis, (e[0][:, :K], e[1][:, :K]))
            for tab, z, e_part in ((tab_re, weighted[0], e[0]), (tab_im, weighted[1], e[1])):
                whole = jnp.concatenate([z, e_part[:, K:]], axis=1)
                for q in range(chunks):
                    tab[pl.ds(q * 8 * CAP + place, CAP, stride=8), :] = whole[:, q * 128 : (q + 1) * 128]
        eight_re[...] = e8[0]
        eight_im[...] = e8[1]
        for c in range(CAP):
            base = tuple(
                jnp.concatenate(
                    [tab[(q * CAP + c) * 8 : (q * CAP + c + 1) * 8, :] for q in range(chunks)], axis=1
                )
                for tab in (tab_re, tab_im)
            )
            c8 = jnp.broadcast_to(eight_re[c : c + 1, :], (8, 2 * K))
            s8 = jnp.broadcast_to(eight_im[c : c + 1, :], (8, 2 * K))
            cc, ss, cs, sc = base[0] * c8, base[1] * s8, base[0] * s8, base[1] * c8
            up = (cc - ss, sc + cs)
            down = (cc + ss, sc - cs)
            down2 = (down[0] * c8 + down[1] * s8, down[1] * c8 - down[0] * s8)
            order = (up, base, down, down2) if mirrored else (down2, down, base, up)
            re = jnp.concatenate([z[0] for z in order], axis=0).astype(jnp.bfloat16)
            im = jnp.concatenate([z[1] for z in order], axis=0).astype(jnp.bfloat16)
            left = jnp.concatenate([re[:, K:], im[:, K:]], axis=1)
            right = jnp.concatenate(
                [
                    jnp.concatenate([re[:, :K], -im[:, :K]], axis=1),
                    empty,
                    jnp.concatenate([im[:, :K], re[:, :K]], axis=1),
                    empty,
                ],
                axis=0,
            )
            cells = dot_last(left, right)
            offset = offset_smem[1 if mirrored else 0, peer * CAP + c]
            row = pl.multiple_of((offset >> 6) * S, S)
            shift = offset & (N2 - 1)
            upper, lower = cells[:HALF], cells[HALF:]
            upper1 = pltpu.roll(upper, shift, 1)
            upper2 = pltpu.roll(upper, shift + N2, 1)
            lower1 = pltpu.roll(lower, shift, 1)
            lower2 = pltpu.roll(lower, shift + N2, 1)
            even = jnp.where(first_half, upper1, lower2)
            odd = jnp.where(first_half, upper2, lower1)
            stays = lane_in >= shift
            sign = -1.0 if mirrored else 1.0
            grid_ref[pl.ds(row, HALF), :] += jnp.where(stays, even, 0.0)
            grid_ref[pl.ds(row + HALF, HALF), :] += sign * jnp.where(stays, odd, 0.0)
            grid_ref[pl.ds(row + S, HALF), :] += jnp.where(stays, 0.0, odd)
            grid_ref[pl.ds(row + S + HALF, HALF), :] += sign * jnp.where(stays, 0.0, even)

    def both(b, _):
        one_list(own + b, False)
        one_list(mirror + b, True)
        return 0

    lax.fori_loop(0, band_count, both, 0)

    def out_copy(part, group):
        rows = pl.ds(group * 8 * N2, 8 * N2)
        return pltpu.make_async_copy(
            rows_ref.at[part, rows, :], out_ref.at[part, rows, :], out_sem.at[part, group]
        )

    twist_re, twist_im = twist_ref[0], twist_ref[1]
    for pair in range(HALF // 2):
        lines = (2 * pair, 2 * pair + 1)
        field = jnp.concatenate(
            [
                jnp.concatenate(
                    [
                        grid_ref[pl.ds(part * HALF + y, N1, stride=S), :].astype(jnp.bfloat16)
                        for y in lines
                    ],
                    axis=1,
                )
                for part in range(2)
            ],
            axis=0,
        )
        section = jnp.dot(outer_ref[...], field, preferred_element_type=jnp.float32)
        twisted = []
        for p in range(2):
            re = section[:N1, p * 128 : (p + 1) * 128]
            im = section[N1:, p * 128 : (p + 1) * 128]
            twisted.append(
                jnp.concatenate(
                    [re * twist_re - im * twist_im, re * twist_im + im * twist_re], axis=1
                ).astype(jnp.bfloat16)
            )
        spectrum = dot_last(inner_ref[...], jnp.concatenate(twisted, axis=0))
        for part in range(2):
            for half in range(2):
                for p, y in enumerate(lines):
                    start = (part * 2 + half) * N2
                    line = half * HALF + y
                    rows_ref[part, pl.ds((line // 8) * 8 * N2 + line % 8, N2, stride=8), :] = spectrum[
                        start : start + N2, p * 128 : (p + 1) * 128
                    ]
        if lines[1] % 8 == 7:
            for part in range(2):
                for half in range(2):
                    out_copy(part, half * (HALF // 8) + lines[1] // 8).start()
    for part in range(2):
        for group in range(S // 8):
            out_copy(part, group).wait()


def shards(visibilities, coordinates, block_index, counts, col_offset):
    band_count = lax.axis_size("band")
    group_count = lax.axis_size("wgrp")
    peers = 2 * band_count
    vmem = pl.BlockSpec(memory_space=pltpu.VMEM)
    message = pl.pallas_call(
        functools.partial(pack_kernel, band_count, group_count),
        out_shape=jax.ShapeDtypeStruct((peers, CAP, ROW), jnp.bfloat16),
        in_specs=[vmem] * 5,
        out_specs=vmem,
        compiler_params=pltpu.CompilerParams(vmem_limit_bytes=40 * 2**20),
        name="pack_blocks",
    )(visibilities[0], coordinates[0], block_index, counts, col_offset)
    groups = [
        [b * group_count + q for b in range(band_count)]
        + [b * group_count + group_count - 1 - q for b in range(band_count)]
        for q in range(group_count // 2)
    ]
    received = lax.all_to_all(
        message, ("band", "wgrp"), 0, 0, axis_index_groups=groups, tiled=True
    )
    outer, inner, twist = transform_tables()
    slots = peers * CAP
    rows = pl.pallas_call(
        functools.partial(grid_kernel, band_count, group_count),
        out_shape=jax.ShapeDtypeStruct((2, S * N2, N1), jnp.float32),
        in_specs=[vmem] * 4,
        out_specs=pl.BlockSpec(memory_space=pl.ANY),
        scratch_shapes=[
            pltpu.VMEM((8, slots), jnp.int32),
            pltpu.SMEM((8, slots), jnp.int32),
            pltpu.VMEM((2 * K // 128 * 8 * CAP, 128), jnp.float32),
            pltpu.VMEM((2 * K // 128 * 8 * CAP, 128), jnp.float32),
            pltpu.VMEM((CAP, 2 * K), jnp.float32),
            pltpu.VMEM((CAP, 2 * K), jnp.float32),
            pltpu.VMEM(((N1 + 2) * S, 128), jnp.float32),
            pltpu.VMEM((2, S * N2, N1), jnp.float32),
            pltpu.SemaphoreType.DMA(()),
            pltpu.SemaphoreType.DMA((2, S // 8)),
        ],
        compiler_params=pltpu.CompilerParams(vmem_limit_bytes=40 * 2**20),
        name="grid_and_transform",
    )(received, outer, inner, twist)
    lines = rows.reshape(1, 2, S // 8, N2, 8, N1).transpose(0, 1, 2, 4, 3, 5)
    return lines.reshape(1, 2, S, G)


def solution(mesh):
    placed = (
        P("wgrp", "band", None),
        P("wgrp", "band", None),
        P("wgrp", "band"),
        P("wgrp", "band"),
        P("wgrp", "band"),
    )
    return jax.shard_map(
        shards, mesh=mesh, in_specs=placed, out_specs=P("wgrp", None, "band", None), check_vma=False
    )
```

profile of v0, /device:TPU:1, one launch (start us, length us, event | category | flops | bytes accessed | tf_op | source)
XLA Modules:
  0.0 35.7 jit_solution(17110151672435912310)
XLA Ops:
  0.0 0.0 copy-start.3
  0.0 0.8 %copy-done.3 = bf16[1,64,512]{2,1,0:T(8,128)(2,1)S(1)} copy-done((bf16[1,64,512]{2,1,0:T(8,128)(2,1)S(1)}, bf16[1,64,512]{2,1,0:T(8,128)(2,1)}, u32[]{:S(2)}) %copy-start.3) | copy-done | bytes 65560
  0.8 0.0 copy-start.4
  0.8 0.8 %copy-done.4 = bf16[1,64,512]{2,1,0:T(8,128)(2,1)S(1)} copy-done((bf16[1,64,512]{2,1,0:T(8,128)(2,1)S(1)}, bf16[1,64,512]{2,1,0:T(8,128)(2,1)}, u32[]{:S(2)}) %copy-start.4) | copy-done | bytes 65560
  1.7 0.0 copy-start.5
  1.7 0.7 %copy-done.5 = s32[1,64]{1,0:T(1,128)S(1)} copy-done((s32[1,64]{1,0:T(1,128)S(1)}, s32[1,64]{1,0:T(1,128)}, u32[]{:S(2)}) %copy-start.5) | copy-done | bytes 280
  2.3 0.0 copy-start.6
  2.3 0.7 %copy-done.6 = s32[1,8]{1,0:T(1,128)S(1)} copy-done((s32[1,8]{1,0:T(1,128)S(1)}, s32[1,8]{1,0:T(1,128)}, u32[]{:S(2)}) %copy-start.6) | copy-done | bytes 56
  3.0 0.0 copy-start.7
  3.0 0.7 %copy-done.7 = s32[1,64]{1,0:T(1,128)S(1)} copy-done((s32[1,64]{1,0:T(1,128)S(1)}, s32[1,64]{1,0:T(1,128)}, u32[]{:S(2)}) %copy-start.7) | copy-done | bytes 280
  3.6 0.3 pack_blocks.1
  4.0 18.4 %all_to_all.5.recv_ref = bf16[16,8,1152]{2,1,0:T(8,128)(2,1)S(1)} all-to-all(bf16[16,8,1152]{2,1,0:T(8,128)(2,1)S(1)} %pack_blocks.1), channel_id=1, replica_groups={{0,4,8,12,16,20,24,28,3,7,11,15,19,23,27,31},{1,5,9,13,17,21,25,29,2,6,..., dimensions={0} | all-to-all | bytes 589824 | tf_op jit(solution)/shard_map/all_to_all | solution.py:312
  22.4 0.0 copy-start
  22.4 0.9 %copy-done = f32[2,128,128]{2,1,0:T(8,128)S(1)} copy-done((f32[2,128,128]{2,1,0:T(8,128)S(1)}, f32[2,128,128]{2,1,0:T(8,128)}, u32[]{:S(2)}) %copy-start) | copy-done | bytes 131096
  23.3 0.0 copy-start.1
  23.3 0.9 %copy-done.1 = bf16[256,256]{1,0:T(8,128)(2,1)S(1)} copy-done((bf16[256,256]{1,0:T(8,128)(2,1)S(1)}, bf16[256,256]{1,0:T(8,128)(2,1)}, u32[]{:S(2)}) %copy-start.1) | copy-done | bytes 131096
  24.2 0.0 copy-start.2
  24.2 0.9 %copy-done.2 = bf16[256,256]{1,0:T(8,128)(2,1)S(1)} copy-done((bf16[256,256]{1,0:T(8,128)(2,1)S(1)}, bf16[256,256]{1,0:T(8,128)(2,1)}, u32[]{:S(2)}) %copy-start.2) | copy-done | bytes 131096
  25.2 10.5 %grid_and_transform.1 = f32[2,2048,128]{2,1,0:T(8,128)} custom-call(bf16[16,8,1152]{2,1,0:T(8,128)(2,1)S(1)} %all_to_all.5.recv_ref, bf16[256,256]{1,0:T(8,128)(2,1)S(1)} %copy-done.2, bf16[256,256]{1,0:T(8,128)(2,1)S(1)} %copy-done.1, f32[2,128,128]{2,1,0:T(8,128)S(1)} %copy-done), custom_call_target="tpu_custom_call" | custom-call | tf_op jit(solution)/shard_map/grid_and_transform/pallas_call | solution.py:317
Async XLA Ops:
  0.0 0.8 %copy-start.3 = (bf16[1,64,512]{2,1,0:T(8,128)(2,1)S(1)}, bf16[1,64,512]{2,1,0:T(8,128)(2,1)}, u32[]{:S(2)}) copy-start(bf16[1,64,512]{2,1,0:T(8,128)(2,1)} %param.8) | copy-start | bytes 196612
  0.8 0.8 %copy-start.4 = (bf16[1,64,512]{2,1,0:T(8,128)(2,1)S(1)}, bf16[1,64,512]{2,1,0:T(8,128)(2,1)}, u32[]{:S(2)}) copy-start(bf16[1,64,512]{2,1,0:T(8,128)(2,1)} %param.9) | copy-start | bytes 196612
  1.7 0.7 %copy-start.5 = (s32[1,64]{1,0:T(1,128)S(1)}, s32[1,64]{1,0:T(1,128)}, u32[]{:S(2)}) copy-start(s32[1,64]{1,0:T(1,128)} %block_ref.1) | copy-start | bytes 772
  2.3 0.7 %copy-start.6 = (s32[1,8]{1,0:T(1,128)S(1)}, s32[1,8]{1,0:T(1,128)}, u32[]{:S(2)}) copy-start(s32[1,8]{1,0:T(1,128)} %count_ref.1) | copy-start | bytes 100
  3.0 0.7 %copy-start.7 = (s32[1,64]{1,0:T(1,128)S(1)}, s32[1,64]{1,0:T(1,128)}, u32[]{:S(2)}) copy-start(s32[1,64]{1,0:T(1,128)} %offset_ref.1) | copy-start | bytes 772
  22.4 0.9 %copy-start = (f32[2,128,128]{2,1,0:T(8,128)S(1)}, f32[2,128,128]{2,1,0:T(8,128)}, u32[]{:S(2)}) copy-start(f32[2,128,128]{2,1,0:T(8,128)} %constant.8.clone.twist_ref) | copy-start | bytes 393220
  23.3 0.9 %copy-start.1 = (bf16[256,256]{1,0:T(8,128)(2,1)S(1)}, bf16[256,256]{1,0:T(8,128)(2,1)}, u32[]{:S(2)}) copy-start(bf16[256,256]{1,0:T(8,128)(2,1)} %constant.7.clone.inner_ref) | copy-start | bytes 393220
  24.2 0.9 %copy-start.2 = (bf16[256,256]{1,0:T(8,128)(2,1)S(1)}, bf16[256,256]{1,0:T(8,128)(2,1)}, u32[]{:S(2)}) copy-start(bf16[256,256]{1,0:T(8,128)(2,1)} %constant.6.clone.outer_ref) | copy-start | bytes 393220
where the time goes:
time: 36.4 us; the launch traced here: 35.7 us
  blocking collectives  18.4 us (51%)
  Pallas kernels  10.9 us (30%)
  local copies, waits for them, and re-layouts  6.35 us (17%)
    all_to_all x1, blocking collectives, shards(): lax.all_to_all(message, ('band', 'wgrp'), 0, 0, axis_index_groups=groups,...  18.4 us
    pallas_call x1, Pallas kernels, shards(): pl.pallas_call(functools.partial(grid_kernel, band_count, group_count), o...  10.5 us
    unnamed x16, local copies, waits for them, and re-layouts  6.35 us

commit v1 on v0

--- a/solution.py
+++ b/solution.py
@@ -12,6 +12,7 @@
 S = 32
 G = 8192
 K = 256
+GROUP = 4
 CAP = 8
 HALF = S // 2
 N1 = 128
@@ -60,8 +61,18 @@
     return jnp.where(low, 0, band_count), jnp.where(low, band_count, 0)
 
 
-def pack_kernel(band_count, group_count, vis_ref, coord_ref, block_ref, count_ref, offset_ref, out_ref):
+def pack_kernel(band_count, group_count, *refs):
+    sources, out_ref, targets, sems = refs[:5], refs[5], refs[6:11], refs[11]
+    copies = [
+        pltpu.make_async_copy(source, target, sems.at[i])
+        for i, (source, target) in enumerate(zip(sources, targets))
+    ]
+    for copy in copies:
+        copy.start()
+    vis_ref, coord_ref, block_ref, count_ref, offset_ref = targets
     own, mirror = own_base(band_count, group_count)
+    for copy in copies:
+        copy.wait()
     slots = block_ref.shape[1]
     blocks = vis_ref.shape[0]
     lane = lax.broadcasted_iota(jnp.int32, (1, slots), 1)
@@ -121,21 +132,33 @@
     band_count,
     group_count,
     recv_ref,
+    outer_hbm,
+    inner_hbm,
+    twist_hbm,
+    out_ref,
     outer_ref,
     inner_ref,
     twist_ref,
-    out_ref,
     offset_vmem,
     offset_smem,
-    tab_re,
-    tab_im,
-    eight_re,
-    eight_im,
+    own_phasors,
+    mirror_phasors,
+    own_cells,
+    mirror_cells,
     grid_ref,
     rows_ref,
     offset_sem,
+    table_sem,
     out_sem,
 ):
+    tables = [
+        pltpu.make_async_copy(source, target, table_sem.at[i])
+        for i, (source, target) in enumerate(
+            ((outer_hbm, outer_ref), (inner_hbm, inner_ref), (twist_hbm, twist_ref))
+        )
+    ]
+    for table in tables:
+        table.start()
     own, mirror = own_base(band_count, group_count)
     band = lax.axis_index("band")
     peers = 2 * band_count
@@ -157,21 +180,41 @@
     to_smem.start()
 
     def clear(step, _):
-        grid_ref[pl.ds(pl.multiple_of(step * 2 * S, 2 * S), 2 * S), :] = jnp.zeros(
-            (2 * S, 128), jnp.float32
-        )
+        for block in range(S // 8):
+            grid_ref[block, pl.ds(pl.multiple_of(step * 16, 16), 16), :] = jnp.zeros(
+                (16, 128), jnp.float32
+            )
         return 0
 
     lax.fori_loop(0, (N1 + 2) // 2, clear, 0)
-    to_smem.wait()
-
-    lane = lax.broadcasted_iota(jnp.int32, (HALF, 128), 1)
+
+    lane = lax.broadcasted_iota(jnp.int32, (8, 128), 1)
     first_half = lane < N2
     lane_in = lane & (N2 - 1)
-    empty = jnp.zeros((S, 2 * K), jnp.bfloat16)
     chunks = 2 * K // 128
-
-    def one_list(peer, mirrored):
+    phasors, cells_ref = (own_phasors, mirror_phasors), (own_cells, mirror_cells)
+
+    def add_cells(cells, start, offset, negate):
+        row = pl.multiple_of((offset >> 6) * 8, 8)
+        shift = offset & (N2 - 1)
+        near, far = (shift + 128 - start) & 127, (shift + N2 - start) & 127
+        stays = (lane_in >= shift) & (lane_in < shift + S)
+        wraps = lane_in < shift - (N2 - S)
+        for block in range(HALF // 8):
+            upper = cells[block * 8 : block * 8 + 8]
+            lower = cells[HALF + block * 8 : HALF + block * 8 + 8]
+            even = jnp.where(first_half, pltpu.roll(upper, near, 1), pltpu.roll(lower, far, 1))
+            odd = jnp.where(first_half, pltpu.roll(upper, far, 1), pltpu.roll(lower, near, 1))
+            for part, here, over in ((0, even, odd), (1, odd, even)):
+                for at, piece in ((row, jnp.where(stays, here, 0.0)), (row + 8, jnp.where(wraps, over, 0.0))):
+                    rows = pl.ds(at, 8)
+                    old = grid_ref[part * (HALF // 8) + block, rows, :]
+                    grid_ref[part * (HALF // 8) + block, rows, :] = (
+                        old - piece if part == 1 and negate else old + piece
+                    )
+
+    def make_tables(peer, mirrored):
+        tab_re, tab_im, eight_re, eight_im = phasors[mirrored]
         block = recv_ref[peer].astype(jnp.float32)
         vis = (block[:, 0:K], block[:, K : 2 * K])
         e1 = unit_phasor(block[:, 2 * K : 4 * K] * (1.0 / S))
@@ -182,64 +225,76 @@
         steps = (one, e1, e2, e3, e4, times(e4, e1), square(e3), times(e4, e3))
         e8 = square(e4)
         for b, e in enumerate(steps):
-            place = CAP - 1 - b if mirrored else b
+            at = CAP - 1 - b if mirrored else b
             weighted = vis if b == 0 else times(vis, (e[0][:, :K], e[1][:, :K]))
             for tab, z, e_part in ((tab_re, weighted[0], e[0]), (tab_im, weighted[1], e[1])):
                 whole = jnp.concatenate([z, e_part[:, K:]], axis=1)
                 for q in range(chunks):
-                    tab[pl.ds(q * 8 * CAP + place, CAP, stride=8), :] = whole[:, q * 128 : (q + 1) * 128]
+                    tab[pl.ds(q * 8 * CAP + at, CAP, stride=8), :] = whole[:, q * 128 : (q + 1) * 128]
         eight_re[...] = e8[0]
         eight_im[...] = e8[1]
+
+    def multiply(mirrored):
+        tab_re, tab_im, eight_re, eight_im = phasors[mirrored]
+        for first in range(0, CAP, GROUP):
+            left, real, imag = [], [], []
+            for c in range(first, first + GROUP):
+                base = tuple(
+                    jnp.concatenate(
+                        [tab[(q * CAP + c) * 8 : (q * CAP + c + 1) * 8, :] for q in range(chunks)],
+                        axis=1,
+                    )
+                    for tab in (tab_re, tab_im)
+                )
+                c8 = jnp.broadcast_to(eight_re[c : c + 1, :], (8, 2 * K))
+                s8 = jnp.broadcast_to(eight_im[c : c + 1, :], (8, 2 * K))
+                cc, ss, cs, sc = base[0] * c8, base[1] * s8, base[0] * s8, base[1] * c8
+                up = (cc - ss, sc + cs)
+                down = (cc + ss, sc - cs)
+                down2 = (down[0] * c8 + down[1] * s8, down[1] * c8 - down[0] * s8)
+                order = (up, base, down, down2) if mirrored else (down2, down, base, up)
+                re = jnp.concatenate([z[0] for z in order], axis=0).astype(jnp.bfloat16)
+                im = jnp.concatenate([z[1] for z in order], axis=0).astype(jnp.bfloat16)
+                left.append(jnp.concatenate([re[:, K:], im[:, K:]], axis=1))
+                real.append(jnp.concatenate([re[:, :K], -im[:, :K]], axis=1))
+                imag.append(jnp.concatenate([im[:, :K], re[:, :K]], axis=1))
+            right = []
+            for c in range(0, GROUP, 2):
+                right += real[c : c + 2] + imag[c : c + 2]
+            cells = dot_last(jnp.concatenate(left, axis=0), jnp.concatenate(right, axis=0))
+            for c in range(GROUP):
+                tile = c // 2 * 128
+                cells_ref[mirrored][(first + c) * S : (first + c + 1) * S, :] = cells[
+                    c * S : (c + 1) * S, tile : tile + 128
+                ]
+
+    def add_list(peer, mirrored):
         for c in range(CAP):
-            base = tuple(
-                jnp.concatenate(
-                    [tab[(q * CAP + c) * 8 : (q * CAP + c + 1) * 8, :] for q in range(chunks)], axis=1
-                )
-                for tab in (tab_re, tab_im)
+            add_cells(
+                cells_ref[mirrored][c * S : (c + 1) * S, :],
+                c % 2 * S,
+                offset_smem[mirrored, peer * CAP + c],
+                mirrored == 1,
             )
-            c8 = jnp.broadcast_to(eight_re[c : c + 1, :], (8, 2 * K))
-            s8 = jnp.broadcast_to(eight_im[c : c + 1, :], (8, 2 * K))
-            cc, ss, cs, sc = base[0] * c8, base[1] * s8, base[0] * s8, base[1] * c8
-            up = (cc - ss, sc + cs)
-            down = (cc + ss, sc - cs)
-            down2 = (down[0] * c8 + down[1] * s8, down[1] * c8 - down[0] * s8)
-            order = (up, base, down, down2) if mirrored else (down2, down, base, up)
-            re = jnp.concatenate([z[0] for z in order], axis=0).astype(jnp.bfloat16)
-            im = jnp.concatenate([z[1] for z in order], axis=0).astype(jnp.bfloat16)
-            left = jnp.concatenate([re[:, K:], im[:, K:]], axis=1)
-            right = jnp.concatenate(
-                [
-                    jnp.concatenate([re[:, :K], -im[:, :K]], axis=1),
-                    empty,
-                    jnp.concatenate([im[:, :K], re[:, :K]], axis=1),
-                    empty,
-                ],
-                axis=0,
-            )
-            cells = dot_last(left, right)
-            offset = offset_smem[1 if mirrored else 0, peer * CAP + c]
-            row = pl.multiple_of((offset >> 6) * S, S)
-            shift = offset & (N2 - 1)
-            upper, lower = cells[:HALF], cells[HALF:]
-            upper1 = pltpu.roll(upper, shift, 1)
-            upper2 = pltpu.roll(upper, shift + N2, 1)
-            lower1 = pltpu.roll(lower, shift, 1)
-            lower2 = pltpu.roll(lower, shift + N2, 1)
-            even = jnp.where(first_half, upper1, lower2)
-            odd = jnp.where(first_half, upper2, lower1)
-            stays = lane_in >= shift
-            sign = -1.0 if mirrored else 1.0
-            grid_ref[pl.ds(row, HALF), :] += jnp.where(stays, even, 0.0)
-            grid_ref[pl.ds(row + HALF, HALF), :] += sign * jnp.where(stays, odd, 0.0)
-            grid_ref[pl.ds(row + S, HALF), :] += jnp.where(stays, 0.0, odd)
-            grid_ref[pl.ds(row + S + HALF, HALF), :] += sign * jnp.where(stays, 0.0, even)
-
-    def both(b, _):
-        one_list(own + b, False)
-        one_list(mirror + b, True)
+
+    make_tables(own, 0)
+    to_smem.wait()
+    cells_ref[1][...] = jnp.zeros_like(cells_ref[1])
+
+    def turn(b, _):
+        multiply(0)
+        add_list(mirror + jnp.maximum(b - 1, 0), 1)
+        make_tables(mirror + b, 1)
+        multiply(1)
+        add_list(own + b, 0)
+        make_tables(own + jnp.minimum(b + 1, band_count - 1), 0)
         return 0
 
-    lax.fori_loop(0, band_count, both, 0)
+    lax.fori_loop(0, band_count, turn, 0)
+    add_list(mirror + band_count - 1, 1)
+
+    for table in tables:
+        table.wait()
 
     def out_copy(part, group):
         rows = pl.ds(group * 8 * N2, 8 * N2)
@@ -254,7 +309,9 @@
             [
                 jnp.concatenate(
                     [
-                        grid_ref[pl.ds(part * HALF + y, N1, stride=S), :].astype(jnp.bfloat16)
+                        grid_ref[
+                            part * (HALF // 8) + y // 8, pl.ds(y % 8, N1, stride=8), :
+                        ].astype(jnp.bfloat16)
                         for y in lines
                     ],
                     axis=1,
@@ -296,14 +353,17 @@
     group_count = lax.axis_size("wgrp")
     peers = 2 * band_count
     vmem = pl.BlockSpec(memory_space=pltpu.VMEM)
+    hbm = pl.BlockSpec(memory_space=pltpu.HBM)
+    inputs = (visibilities[0], coordinates[0], block_index, counts, col_offset)
     message = pl.pallas_call(
         functools.partial(pack_kernel, band_count, group_count),
         out_shape=jax.ShapeDtypeStruct((peers, CAP, ROW), jnp.bfloat16),
-        in_specs=[vmem] * 5,
+        in_specs=[hbm] * 5,
         out_specs=vmem,
-        compiler_params=pltpu.CompilerParams(vmem_limit_bytes=40 * 2**20),
+        scratch_shapes=[pltpu.VMEM(a.shape, a.dtype) for a in inputs]
+        + [pltpu.SemaphoreType.DMA((len(inputs),))],
         name="pack_blocks",
-    )(visibilities[0], coordinates[0], block_index, counts, col_offset)
+    )(*inputs)
     groups = [
         [b * group_count + q for b in range(band_count)]
         + [b * group_count + group_count - 1 - q for b in range(band_count)]
@@ -314,24 +374,30 @@
     )
     outer, inner, twist = transform_tables()
     slots = peers * CAP
+    base = pltpu.VMEM((2 * K // 128 * 8 * CAP, 128), jnp.float32)
+    step = pltpu.VMEM((CAP, 2 * K), jnp.float32)
+    phasors = (base, base, step, step)
     rows = pl.pallas_call(
         functools.partial(grid_kernel, band_count, group_count),
         out_shape=jax.ShapeDtypeStruct((2, S * N2, N1), jnp.float32),
-        in_specs=[vmem] * 4,
+        in_specs=[vmem] + [hbm] * 3,
         out_specs=pl.BlockSpec(memory_space=pl.ANY),
         scratch_shapes=[
+            pltpu.VMEM(outer.shape, outer.dtype),
+            pltpu.VMEM(inner.shape, inner.dtype),
+            pltpu.VMEM(twist.shape, twist.dtype),
             pltpu.VMEM((8, slots), jnp.int32),
             pltpu.SMEM((8, slots), jnp.int32),
-            pltpu.VMEM((2 * K // 128 * 8 * CAP, 128), jnp.float32),
-            pltpu.VMEM((2 * K // 128 * 8 * CAP, 128), jnp.float32),
-            pltpu.VMEM((CAP, 2 * K), jnp.float32),
-            pltpu.VMEM((CAP, 2 * K), jnp.float32),
-            pltpu.VMEM(((N1 + 2) * S, 128), jnp.float32),
+            phasors,
+            phasors,
+            pltpu.VMEM((CAP * S, 128), jnp.float32),
+            pltpu.VMEM((CAP * S, 128), jnp.float32),
+            pltpu.VMEM((S // 8, (N1 + 2) * 8, 128), jnp.float32),
             pltpu.VMEM((2, S * N2, N1), jnp.float32),
             pltpu.SemaphoreType.DMA(()),
+            pltpu.SemaphoreType.DMA((3,)),
             pltpu.SemaphoreType.DMA((2, S // 8)),
         ],
-        compiler_params=pltpu.CompilerParams(vmem_limit_bytes=40 * 2**20),
         name="grid_and_transform",
     )(received, outer, inner, twist)
     lines = rows.reshape(1, 2, S // 8, N2, 8, N1).transpose(0, 1, 2, 4, 3, 5)

time: 36.4 us -> 30.1 us (0.83)
  the two profiles are of different devices: /device:TPU:1 before, /device:TPU:0 now
where the time goes in v1:
time: 30.1 us; the launch traced here: 29.8 us
  blocking collectives  19.2 us (64%)
  Pallas kernels  10.7 us (36%)
    all_to_all x1, blocking collectives, shards(): lax.all_to_all(message, ('band', 'wgrp'), 0, 0, axis_index_groups=groups,...  19.2 us
    pallas_call x1, Pallas kernels, shards(): pl.pallas_call(functools.partial(grid_kernel, band_count, group_count), o...  8.7 us
    pallas_call x1, Pallas kernels, shards(): pl.pallas_call(functools.partial(pack_kernel, band_count, group_count), o...  1.98 us

profile of v1, /device:TPU:0, one launch (start us, length us, event | category | flops | bytes accessed | tf_op | source)
XLA Modules:
  0.0 29.8 jit_solution(6083197909477627206)
XLA Ops:
  0.0 2.0 %pack_blocks.1 = bf16[16,8,1152]{2,1,0:T(8,128)(2,1)} custom-call(bf16[64,512]{1,0:T(8,128)(2,1)} %bitcast.7, bf16[64,512]{1,0:T(8,128)(2,1)} %bitcast.8, s32[1,64]{1,0:T(1,128)} %refs_2_.1, s32[1,8]{1,0:T(1,128)} %refs_3_.1, s32[1,64]{1,0:T(1,128)} %refs_4_.1), custom_call_target="tpu_custom_call" | custom-call | tf_op jit(solution)/shard_map/pack_blocks/pallas_call | solution.py:358
  2.0 19.2 %all_to_all.5.recv_ref = bf16[16,8,1152]{2,1,0:T(8,128)(2,1)} all-to-all(bf16[16,8,1152]{2,1,0:T(8,128)(2,1)} %pack_blocks.1), channel_id=1, replica_groups={{0,4,8,12,16,20,24,28,3,7,11,15,19,23,27,31},{1,5,9,13,17,21,25,29,2,6,..., dimensions={0} | all-to-all | bytes 589824 | tf_op jit(solution)/shard_map/all_to_all | solution.py:372
  21.1 8.7 %grid_and_transform.1 = f32[2,2048,128]{2,1,0:T(8,128)} custom-call(bf16[16,8,1152]{2,1,0:T(8,128)(2,1)} %all_to_all.5.recv_ref, bf16[256,256]{1,0:T(8,128)(2,1)} %constant.6.clone.outer_hbm, bf16[256,256]{1,0:T(8,128)(2,1)} %constant.7.clone.inner_hbm, f32[2,128,128]{2,1,0:T(8,128)} %constant.8.clone.twist_hbm), custom_call_target="tpu_custom_call" | custom-call | tf_op jit(solution)/shard_map/grid_and_transform/pallas_call | solution.py:380

commit v2 on v1

--- a/solution.py
+++ b/solution.py
@@ -3,7 +3,6 @@
 
 import jax
 import jax.numpy as jnp
-import numpy as np
 from jax import lax
 from jax.experimental import pallas as pl
 from jax.experimental.pallas import tpu as pltpu
@@ -19,29 +18,12 @@
 N2 = 64
 DATA = 4 * K
 ROW = DATA + 128
+LIVE = 32
 LO = 64
 PI = math.pi
 
 SIN_TERMS = (1.0, -1 / 6, 1 / 120, -1 / 5040, 1 / 362880, -1 / 39916800)
 COS_TERMS = (1.0, -1 / 2, 1 / 24, -1 / 720, 1 / 40320, -1 / 3628800, 1 / 479001600)
-
-
-def transform_tables():
-    n1, n2 = np.arange(N1), np.arange(N2)
-    outer = np.exp(-2j * np.pi * (np.outer(n1, n1) % N1) / N1)
-    inner = np.exp(-2j * np.pi * (np.outer(n2, n2) % N2) / N2)
-    twist = np.exp(-2j * np.pi * np.outer(n1, n2) / G) / math.sqrt(G * K)
-    pair = np.kron(np.eye(2), inner)
-
-    def real_form(m):
-        return np.block([[m.real, -m.imag], [m.imag, m.real]])
-
-    twist = np.concatenate([twist, twist], axis=1)
-    return (
-        jnp.asarray(real_form(outer), jnp.bfloat16),
-        jnp.asarray(real_form(pair), jnp.bfloat16),
-        jnp.asarray(np.stack([twist.real, twist.imag]), jnp.float32),
-    )
 
 
 def dot_last(left, right):
@@ -96,8 +78,12 @@
     column = lax.broadcasted_iota(jnp.int32, (slots, 128), 1)
     to_high = (slot_row == column).astype(jnp.bfloat16)
     to_low = (slot_row + LO == column).astype(jnp.bfloat16)
-    meta = jnp.dot(high, to_high, preferred_element_type=jnp.float32) + jnp.dot(
-        low, to_low, preferred_element_type=jnp.float32
+    to_live = (slot_row + LIVE == column).astype(jnp.bfloat16)
+    alive = jnp.where(here, live, 0.0).astype(jnp.bfloat16)
+    meta = (
+        jnp.dot(high, to_high, preferred_element_type=jnp.float32)
+        + jnp.dot(low, to_low, preferred_element_type=jnp.float32)
+        + jnp.dot(alive, to_live, preferred_element_type=jnp.float32)
     )
     for d in range(band_count):
         rows = slice(d * CAP, (d + 1) * CAP)
@@ -128,54 +114,95 @@
     return 1.0 - 2.0 * (sine * sine), 2.0 * (sine * cosine)
 
 
+def turns(rows, columns, length):
+    return unit_phasor(((rows * columns) & (length - 1)).astype(jnp.float32) * (1.0 / length))
+
+
+def fill_tables(outer_ref, inner_ref, twist_ref):
+    row = lax.broadcasted_iota(jnp.int32, (N1, 128), 0)
+    column = lax.broadcasted_iota(jnp.int32, (N1, 128), 1)
+    row_in, column_in = row & (N2 - 1), column & (N2 - 1)
+    outer = turns(row, column, N1)
+    same = (row ^ column) < N2
+    inner = [jnp.where(same, z, 0.0) for z in turns(row_in, column_in, N2)]
+    for ref, (cosine, sine) in ((outer_ref, outer), (inner_ref, inner)):
+        cosine, sine = cosine.astype(jnp.bfloat16), sine.astype(jnp.bfloat16)
+        ref[:N1, :128] = cosine
+        ref[:N1, 128:] = sine
+        ref[N1:, :128] = -sine
+        ref[N1:, 128:] = cosine
+    scale = 1.0 / math.sqrt(G * K)
+    twist = turns(row, column_in, G)
+    twist_ref[0] = twist[0] * scale
+    twist_ref[1] = twist[1] * -scale
+
+
 def grid_kernel(
     band_count,
     group_count,
     recv_ref,
-    outer_hbm,
-    inner_hbm,
-    twist_hbm,
     out_ref,
     outer_ref,
     inner_ref,
     twist_ref,
     offset_vmem,
     offset_smem,
-    own_phasors,
-    mirror_phasors,
-    own_cells,
-    mirror_cells,
+    data_ref,
+    tab_re,
+    tab_im,
+    eight_re,
+    eight_im,
+    cells_ref,
     grid_ref,
     rows_ref,
     offset_sem,
-    table_sem,
     out_sem,
 ):
-    tables = [
-        pltpu.make_async_copy(source, target, table_sem.at[i])
-        for i, (source, target) in enumerate(
-            ((outer_hbm, outer_ref), (inner_hbm, inner_ref), (twist_hbm, twist_ref))
-        )
-    ]
-    for table in tables:
-        table.start()
-    own, mirror = own_base(band_count, group_count)
+    own, _ = own_base(band_count, group_count)
     band = lax.axis_index("band")
-    peers = 2 * band_count
-
-    meta = recv_ref[:, :, DATA:].astype(jnp.float32).reshape(peers * CAP, 128)
+
+    slots = 2 * band_count * CAP
+    flat = recv_ref[...].astype(jnp.float32).reshape(slots, ROW).astype(jnp.bfloat16)
     pick_row = lax.broadcasted_iota(jnp.int32, (8, 128), 0)
     pick_col = lax.broadcasted_iota(jnp.int32, (8, 128), 1)
     flipped = band_count - 1 - band
-    wanted = jnp.where(
-        pick_row == 0,
-        band,
-        jnp.where(pick_row == 1, band + LO, jnp.where(pick_row == 2, flipped, flipped + LO)),
-    )
-    pick = (pick_col == wanted).astype(jnp.bfloat16)
-    picked = dot_last(pick, meta.astype(jnp.bfloat16))
-    offset_vmem[0:1] = (picked[0:1] * 128.0 + picked[1:2]).astype(jnp.int32)
-    offset_vmem[1:2] = (G - S) - (picked[2:3] * 128.0 + picked[3:4]).astype(jnp.int32)
+    wanted = jnp.full((8, 128), -1, jnp.int32)
+    for i, at in enumerate((0, LO, LIVE)):
+        wanted = jnp.where(pick_row == i, band + at, wanted)
+        wanted = jnp.where(pick_row == i + 3, flipped + at, wanted)
+    picked = dot_last((pick_col == wanted).astype(jnp.bfloat16), flat[:, DATA:])
+    slot = lax.broadcasted_iota(jnp.int32, (1, slots), 1)
+    mine = (slot >= own * CAP) & (slot < (own + band_count) * CAP)
+    high, low, live = (jnp.where(mine, picked[i : i + 1], picked[i + 3 : i + 4]) for i in range(3))
+    offsets = (high * 128.0 + low).astype(jnp.int32)
+    offsets = jnp.where(mine, offsets, (G - S) - offsets)
+
+    live_own = jnp.where(mine, live, 0.0)
+    live_mirror = live - live_own
+    nothing = jnp.zeros((6, slots), jnp.float32)
+    kinds = jnp.concatenate([live_own, live_mirror, nothing], axis=0).astype(jnp.bfloat16)
+    earlier = (
+        lax.broadcasted_iota(jnp.int32, (slots, slots), 0)
+        < lax.broadcasted_iota(jnp.int32, (slots, slots), 1)
+    ).astype(jnp.bfloat16)
+    before = jnp.dot(kinds, earlier, preferred_element_type=jnp.float32)
+    own_groups, mirror_groups = (
+        jnp.floor((jnp.sum(z, axis=1, keepdims=True) + (CAP - 1)) * (1.0 / CAP))
+        for z in (live_own, live_mirror)
+    )
+    position = jnp.where(mine, before[0:1], before[1:2] + CAP * own_groups)
+    position = jnp.where(live > 0.5, position, -1.0).astype(jnp.int32)
+    moves = (
+        lax.broadcasted_iota(jnp.int32, (slots, slots), 0) == position
+    ).astype(jnp.bfloat16)
+    data_ref[...] = jnp.dot(moves, flat[:, :DATA], preferred_element_type=jnp.float32)
+    parts = jnp.concatenate(
+        [(offsets >> 7).astype(jnp.float32), (offsets & 127).astype(jnp.float32), nothing], axis=0
+    )
+    moved = dot_last(parts.astype(jnp.bfloat16), moves)
+    offset_vmem[0:1] = (moved[0:1] * 128.0 + moved[1:2]).astype(jnp.int32)
+    offset_vmem[1:2] = jnp.broadcast_to(own_groups, (1, slots)).astype(jnp.int32)
+    offset_vmem[2:3] = jnp.broadcast_to(own_groups + mirror_groups, (1, slots)).astype(jnp.int32)
     to_smem = pltpu.make_async_copy(offset_vmem, offset_smem, offset_sem)
     to_smem.start()
 
@@ -192,9 +219,8 @@
     first_half = lane < N2
     lane_in = lane & (N2 - 1)
     chunks = 2 * K // 128
-    phasors, cells_ref = (own_phasors, mirror_phasors), (own_cells, mirror_cells)
-
-    def add_cells(cells, start, offset, negate):
+
+    def add_cells(cells, start, offset):
         row = pl.multiple_of((offset >> 6) * 8, 8)
         shift = offset & (N2 - 1)
         near, far = (shift + 128 - start) & 127, (shift + N2 - start) & 127
@@ -208,25 +234,21 @@
             for part, here, over in ((0, even, odd), (1, odd, even)):
                 for at, piece in ((row, jnp.where(stays, here, 0.0)), (row + 8, jnp.where(wraps, over, 0.0))):
                     rows = pl.ds(at, 8)
-                    old = grid_ref[part * (HALF // 8) + block, rows, :]
-                    grid_ref[part * (HALF // 8) + block, rows, :] = (
-                        old - piece if part == 1 and negate else old + piece
-                    )
-
-    def make_tables(peer, mirrored):
-        tab_re, tab_im, eight_re, eight_im = phasors[mirrored]
-        block = recv_ref[peer].astype(jnp.float32)
-        vis = (block[:, 0:K], block[:, K : 2 * K])
+                    grid_ref[part * (HALF // 8) + block, rows, :] += piece
+
+    def make_tables(group, mirrored):
+        block = data_ref[pl.ds(pl.multiple_of(group * CAP, CAP), CAP), :]
+        flip = jnp.where(mirrored == 1, -1.0, 1.0)
+        vis = (block[:, 0:K], block[:, K : 2 * K] * flip)
         e1 = unit_phasor(block[:, 2 * K : 4 * K] * (1.0 / S))
         e2 = square(e1)
         e3 = times(e2, e1)
         e4 = square(e2)
-        one = (jnp.ones_like(e1[0]), jnp.zeros_like(e1[0]))
-        steps = (one, e1, e2, e3, e4, times(e4, e1), square(e3), times(e4, e3))
         e8 = square(e4)
-        for b, e in enumerate(steps):
-            at = CAP - 1 - b if mirrored else b
-            weighted = vis if b == 0 else times(vis, (e[0][:, :K], e[1][:, :K]))
+        edge = tuple(jnp.where(mirrored == 1, z, one) for z, one in zip(e8, (1.0, 0.0)))
+        for b, e in enumerate((edge, e1, e2, e3, e4, times(e4, e1), square(e3), times(e4, e3))):
+            at = 7 * mirrored if b == 0 else b - mirrored
+            weighted = times(vis, (e[0][:, :K], e[1][:, :K]))
             for tab, z, e_part in ((tab_re, weighted[0], e[0]), (tab_im, weighted[1], e[1])):
                 whole = jnp.concatenate([z, e_part[:, K:]], axis=1)
                 for q in range(chunks):
@@ -234,8 +256,7 @@
         eight_re[...] = e8[0]
         eight_im[...] = e8[1]
 
-    def multiply(mirrored):
-        tab_re, tab_im, eight_re, eight_im = phasors[mirrored]
+    def multiply():
         for first in range(0, CAP, GROUP):
             left, real, imag = [], [], []
             for c in range(first, first + GROUP):
@@ -252,7 +273,7 @@
                 up = (cc - ss, sc + cs)
                 down = (cc + ss, sc - cs)
                 down2 = (down[0] * c8 + down[1] * s8, down[1] * c8 - down[0] * s8)
-                order = (up, base, down, down2) if mirrored else (down2, down, base, up)
+                order = (down2, down, base, up)
                 re = jnp.concatenate([z[0] for z in order], axis=0).astype(jnp.bfloat16)
                 im = jnp.concatenate([z[1] for z in order], axis=0).astype(jnp.bfloat16)
                 left.append(jnp.concatenate([re[:, K:], im[:, K:]], axis=1))
@@ -264,37 +285,29 @@
             cells = dot_last(jnp.concatenate(left, axis=0), jnp.concatenate(right, axis=0))
             for c in range(GROUP):
                 tile = c // 2 * 128
-                cells_ref[mirrored][(first + c) * S : (first + c + 1) * S, :] = cells[
+                cells_ref[(first + c) * S : (first + c + 1) * S, :] = cells[
                     c * S : (c + 1) * S, tile : tile + 128
                 ]
 
-    def add_list(peer, mirrored):
+    def add_group(group):
         for c in range(CAP):
-            add_cells(
-                cells_ref[mirrored][c * S : (c + 1) * S, :],
-                c % 2 * S,
-                offset_smem[mirrored, peer * CAP + c],
-                mirrored == 1,
-            )
-
-    make_tables(own, 0)
+            add_cells(cells_ref[c * S : (c + 1) * S, :], c % 2 * S, offset_smem[0, group * CAP + c])
+
+    make_tables(0, jnp.int32(0))
+    fill_tables(outer_ref, inner_ref, twist_ref)
+    cells_ref[...] = jnp.zeros_like(cells_ref)
     to_smem.wait()
-    cells_ref[1][...] = jnp.zeros_like(cells_ref[1])
-
-    def turn(b, _):
-        multiply(0)
-        add_list(mirror + jnp.maximum(b - 1, 0), 1)
-        make_tables(mirror + b, 1)
-        multiply(1)
-        add_list(own + b, 0)
-        make_tables(own + jnp.minimum(b + 1, band_count - 1), 0)
+    first_mirrored, groups = offset_smem[1, 0], offset_smem[2, 0]
+
+    def turn(group, _):
+        add_group(jnp.maximum(group - 1, 0))
+        multiply()
+        later = jnp.minimum(group + 1, groups - 1)
+        make_tables(later, (later >= first_mirrored).astype(jnp.int32))
         return 0
 
-    lax.fori_loop(0, band_count, turn, 0)
-    add_list(mirror + band_count - 1, 1)
-
-    for table in tables:
-        table.wait()
+    lax.fori_loop(0, groups, turn, 0)
+    add_group(groups - 1)
 
     def out_copy(part, group):
         rows = pl.ds(group * 8 * N2, 8 * N2)
@@ -372,34 +385,34 @@
     received = lax.all_to_all(
         message, ("band", "wgrp"), 0, 0, axis_index_groups=groups, tiled=True
     )
-    outer, inner, twist = transform_tables()
     slots = peers * CAP
     base = pltpu.VMEM((2 * K // 128 * 8 * CAP, 128), jnp.float32)
     step = pltpu.VMEM((CAP, 2 * K), jnp.float32)
-    phasors = (base, base, step, step)
     rows = pl.pallas_call(
         functools.partial(grid_kernel, band_count, group_count),
         out_shape=jax.ShapeDtypeStruct((2, S * N2, N1), jnp.float32),
-        in_specs=[vmem] + [hbm] * 3,
+        in_specs=[vmem],
         out_specs=pl.BlockSpec(memory_space=pl.ANY),
         scratch_shapes=[
-            pltpu.VMEM(outer.shape, outer.dtype),
-            pltpu.VMEM(inner.shape, inner.dtype),
-            pltpu.VMEM(twist.shape, twist.dtype),
+            pltpu.VMEM((2 * N1, 256), jnp.bfloat16),
+            pltpu.VMEM((2 * N1, 256), jnp.bfloat16),
+            pltpu.VMEM((2, N1, 128), jnp.float32),
             pltpu.VMEM((8, slots), jnp.int32),
             pltpu.SMEM((8, slots), jnp.int32),
-            phasors,
-            phasors,
-            pltpu.VMEM((CAP * S, 128), jnp.float32),
+            pltpu.VMEM((slots, DATA), jnp.float32),
+            base,
+            base,
+            step,
+            step,
             pltpu.VMEM((CAP * S, 128), jnp.float32),
             pltpu.VMEM((S // 8, (N1 + 2) * 8, 128), jnp.float32),
             pltpu.VMEM((2, S * N2, N1), jnp.float32),
             pltpu.SemaphoreType.DMA(()),
-            pltpu.SemaphoreType.DMA((3,)),
             pltpu.SemaphoreType.DMA((2, S // 8)),
         ],
+        compiler_params=pltpu.CompilerParams(vmem_limit_bytes=48 * 2**20),
         name="grid_and_transform",
-    )(received, outer, inner, twist)
+    )(received)
     lines = rows.reshape(1, 2, S // 8, N2, 8, N1).transpose(0, 1, 2, 4, 3, 5)
     return lines.reshape(1, 2, S, G)
 

time: 30.1 us -> 28.7 us (0.953)
  Pallas kernels: 10.7 us -> 9.35 us
    pallas_call x1, Pallas kernels: 8.7 us -> 7.36 us  [shards(): pl.pallas_call(functools.partial(grid_kernel, band_count, group_count), o...]
where the time goes in v2:
time: 28.7 us; the launch traced here: 28.4 us
  blocking collectives  19.1 us (67%)
  Pallas kernels  9.35 us (33%)
    all_to_all x1, blocking collectives, shards(): lax.all_to_all(message, ('band', 'wgrp'), 0, 0, axis_index_groups=groups,...  19.1 us
    pallas_call x1, Pallas kernels, shards(): pl.pallas_call(functools.partial(grid_kernel, band_count, group_count), o...  7.36 us
    pallas_call x1, Pallas kernels, shards(): pl.pallas_call(functools.partial(pack_kernel, band_count, group_count), o...  1.99 us

profile of v2, /device:TPU:0, one launch (start us, length us, event | category | flops | bytes accessed | tf_op | source)
XLA Modules:
  0.0 28.4 jit_solution(10796517182871141274)
XLA Ops:
  0.0 2.0 %pack_blocks.1 = bf16[16,8,1152]{2,1,0:T(8,128)(2,1)} custom-call(bf16[64,512]{1,0:T(8,128)(2,1)} %bitcast.7, bf16[64,512]{1,0:T(8,128)(2,1)} %bitcast.8, s32[1,64]{1,0:T(1,128)} %refs_2_.1, s32[1,8]{1,0:T(1,128)} %refs_3_.1, s32[1,64]{1,0:T(1,128)} %refs_4_.1), custom_call_target="tpu_custom_call" | custom-call | tf_op jit(solution)/shard_map/pack_blocks/pallas_call | solution.py:371
  2.0 19.1 %all_to_all.5.recv_ref = bf16[16,8,1152]{2,1,0:T(8,128)(2,1)S(1)} all-to-all(bf16[16,8,1152]{2,1,0:T(8,128)(2,1)} %pack_blocks.1), channel_id=1, replica_groups={{0,4,8,12,16,20,24,28,3,7,11,15,19,23,27,31},{1,5,9,13,17,21,25,29,2,6,..., dimensions={0} | all-to-all | bytes 589824 | tf_op jit(solution)/shard_map/all_to_all | solution.py:385
  21.1 7.4 %grid_and_transform.1 = f32[2,2048,128]{2,1,0:T(8,128)} custom-call(bf16[16,8,1152]{2,1,0:T(8,128)(2,1)S(1)} %all_to_all.5.recv_ref), custom_call_target="tpu_custom_call" | custom-call | tf_op jit(solution)/shard_map/grid_and_transform/pallas_call | solution.py:391

commit v3 on v2

--- a/solution.py
+++ b/solution.py
@@ -11,7 +11,7 @@
 S = 32
 G = 8192
 K = 256
-GROUP = 4
+GROUP = 2
 CAP = 8
 HALF = S // 2
 N1 = 128
@@ -22,8 +22,8 @@
 LO = 64
 PI = math.pi
 
-SIN_TERMS = (1.0, -1 / 6, 1 / 120, -1 / 5040, 1 / 362880, -1 / 39916800)
-COS_TERMS = (1.0, -1 / 2, 1 / 24, -1 / 720, 1 / 40320, -1 / 3628800, 1 / 479001600)
+SIN_TERMS = (0.99999999572, -0.1666665797, 0.0083330506173, -0.00019809046357, 2.6051662762e-06)
+COS_TERMS = (0.99999995325, -0.49999905063, 0.041663578931, -0.0013853666933, 2.3153174156e-05)
 
 
 def dot_last(left, right):
@@ -43,34 +43,26 @@
     return jnp.where(low, 0, band_count), jnp.where(low, band_count, 0)
 
 
-def pack_kernel(band_count, group_count, *refs):
-    sources, out_ref, targets, sems = refs[:5], refs[5], refs[6:11], refs[11]
-    copies = [
-        pltpu.make_async_copy(source, target, sems.at[i])
-        for i, (source, target) in enumerate(zip(sources, targets))
-    ]
-    for copy in copies:
-        copy.start()
-    vis_ref, coord_ref, block_ref, count_ref, offset_ref = targets
+def pack_kernel(band_count, group_count, data_ref, whole_ref, out_ref):
     own, mirror = own_base(band_count, group_count)
-    for copy in copies:
-        copy.wait()
-    slots = block_ref.shape[1]
-    blocks = vis_ref.shape[0]
+    slots = band_count * CAP
+    block_index = whole_ref[:, :slots]
+    offsets = whole_ref[:, slots : 2 * slots]
+    count = whole_ref[:, 2 * slots :]
+    blocks = data_ref.shape[0]
     lane = lax.broadcasted_iota(jnp.int32, (1, slots), 1)
     list_of = lane // CAP
     within = lane % CAP
     band_row = lax.broadcasted_iota(jnp.int32, (band_count, slots), 0)
     in_list = (band_row == list_of).astype(jnp.float32)
-    counts = jnp.broadcast_to(count_ref[...].astype(jnp.float32), (8, band_count))
+    counts = jnp.broadcast_to(count.astype(jnp.float32), (8, band_count))
     live_count = jnp.dot(counts, in_list, preferred_element_type=jnp.float32)[0:1]
     live = (within.astype(jnp.float32) < live_count).astype(jnp.float32)
     chosen = (
-        lax.broadcasted_iota(jnp.int32, (blocks, slots), 0) == block_ref[...]
+        lax.broadcasted_iota(jnp.int32, (blocks, slots), 0) == block_index
     ).astype(jnp.float32)
-    vis = dot_first((chosen * live).astype(jnp.bfloat16), vis_ref[...])
-    coord = dot_first(chosen.astype(jnp.bfloat16), coord_ref[...])
-    offsets = offset_ref[...]
+    vis = dot_first((chosen * live).astype(jnp.bfloat16), data_ref[:, : 2 * K])
+    coord = dot_first(chosen.astype(jnp.bfloat16), data_ref[:, 2 * K :])
     here = lax.broadcasted_iota(jnp.int32, (CAP, slots), 0) == within
     high = jnp.where(here, (offsets >> 7).astype(jnp.float32), 0.0).astype(jnp.bfloat16)
     low = jnp.where(here, (offsets & 127).astype(jnp.float32), 0.0).astype(jnp.bfloat16)
@@ -114,17 +106,28 @@
     return 1.0 - 2.0 * (sine * sine), 2.0 * (sine * cosine)
 
 
-def turns(rows, columns, length):
-    return unit_phasor(((rows * columns) & (length - 1)).astype(jnp.float32) * (1.0 / length))
+def turn_table(rows, column, length):
+    row = lax.broadcasted_iota(jnp.int32, column.shape, 0)
+
+    def turns(factor):
+        return unit_phasor(((factor * column) & (length - 1)).astype(jnp.float32) * (1.0 / length))
+
+    parts = [turns(row)]
+    step = turns(jnp.full_like(row, 8))
+    for _ in range(rows // 8 - 1):
+        parts.append(times(parts[-1], step))
+    return tuple(jnp.concatenate([z[i] for z in parts], axis=0) for i in range(2))
 
 
 def fill_tables(outer_ref, inner_ref, twist_ref):
-    row = lax.broadcasted_iota(jnp.int32, (N1, 128), 0)
-    column = lax.broadcasted_iota(jnp.int32, (N1, 128), 1)
-    row_in, column_in = row & (N2 - 1), column & (N2 - 1)
-    outer = turns(row, column, N1)
-    same = (row ^ column) < N2
-    inner = [jnp.where(same, z, 0.0) for z in turns(row_in, column_in, N2)]
+    column = lax.broadcasted_iota(jnp.int32, (8, 128), 1)
+    column_in = column & (N2 - 1)
+    outer = turn_table(N1, column, N1)
+    left = lax.broadcasted_iota(jnp.int32, (N2, 128), 1) < N2
+    inner = [
+        jnp.concatenate([jnp.where(left, z, 0.0), jnp.where(left, 0.0, z)], axis=0)
+        for z in turn_table(N2, column_in, N2)
+    ]
     for ref, (cosine, sine) in ((outer_ref, outer), (inner_ref, inner)):
         cosine, sine = cosine.astype(jnp.bfloat16), sine.astype(jnp.bfloat16)
         ref[:N1, :128] = cosine
@@ -132,7 +135,7 @@
         ref[N1:, :128] = -sine
         ref[N1:, 128:] = cosine
     scale = 1.0 / math.sqrt(G * K)
-    twist = turns(row, column_in, G)
+    twist = turn_table(N1, column_in, G)
     twist_ref[0] = twist[0] * scale
     twist_ref[1] = twist[1] * -scale
 
@@ -242,11 +245,12 @@
         vis = (block[:, 0:K], block[:, K : 2 * K] * flip)
         e1 = unit_phasor(block[:, 2 * K : 4 * K] * (1.0 / S))
         e2 = square(e1)
-        e3 = times(e2, e1)
         e4 = square(e2)
+        cc, ss, cs, sc = e4[0] * e1[0], e4[1] * e1[1], e4[0] * e1[1], e4[1] * e1[0]
+        e3, e5 = (cc + ss, sc - cs), (cc - ss, sc + cs)
         e8 = square(e4)
         edge = tuple(jnp.where(mirrored == 1, z, one) for z, one in zip(e8, (1.0, 0.0)))
-        for b, e in enumerate((edge, e1, e2, e3, e4, times(e4, e1), square(e3), times(e4, e3))):
+        for b, e in enumerate((edge, e1, e2, e3, e4, e5, square(e3), times(e4, e3))):
             at = 7 * mirrored if b == 0 else b - mirrored
             weighted = times(vis, (e[0][:, :K], e[1][:, :K]))
             for tab, z, e_part in ((tab_re, weighted[0], e[0]), (tab_im, weighted[1], e[1])):
@@ -257,6 +261,7 @@
         eight_im[...] = e8[1]
 
     def multiply():
+        products = []
         for first in range(0, CAP, GROUP):
             left, real, imag = [], [], []
             for c in range(first, first + GROUP):
@@ -283,11 +288,13 @@
             for c in range(0, GROUP, 2):
                 right += real[c : c + 2] + imag[c : c + 2]
             cells = dot_last(jnp.concatenate(left, axis=0), jnp.concatenate(right, axis=0))
-            for c in range(GROUP):
-                tile = c // 2 * 128
-                cells_ref[(first + c) * S : (first + c + 1) * S, :] = cells[
-                    c * S : (c + 1) * S, tile : tile + 128
-                ]
+            products.append(cells)
+        return products
+
+    def keep(products):
+        for c in range(CAP):
+            row, tile = c % GROUP * S, c % GROUP // 2 * 128
+            cells_ref[c * S : (c + 1) * S, :] = products[c // GROUP][row : row + S, tile : tile + 128]
 
     def add_group(group):
         for c in range(CAP):
@@ -300,8 +307,9 @@
     first_mirrored, groups = offset_smem[1, 0], offset_smem[2, 0]
 
     def turn(group, _):
+        products = multiply()
         add_group(jnp.maximum(group - 1, 0))
-        multiply()
+        keep(products)
         later = jnp.minimum(group + 1, groups - 1)
         make_tables(later, (later >= first_mirrored).astype(jnp.int32))
         return 0
@@ -367,16 +375,16 @@
     peers = 2 * band_count
     vmem = pl.BlockSpec(memory_space=pltpu.VMEM)
     hbm = pl.BlockSpec(memory_space=pltpu.HBM)
-    inputs = (visibilities[0], coordinates[0], block_index, counts, col_offset)
+    blocks = jnp.concatenate([visibilities[0], coordinates[0]], axis=1)
+    whole = jnp.concatenate([block_index, col_offset, counts], axis=1)
     message = pl.pallas_call(
         functools.partial(pack_kernel, band_count, group_count),
         out_shape=jax.ShapeDtypeStruct((peers, CAP, ROW), jnp.bfloat16),
-        in_specs=[hbm] * 5,
+        in_specs=[vmem] * 2,
         out_specs=vmem,
-        scratch_shapes=[pltpu.VMEM(a.shape, a.dtype) for a in inputs]
-        + [pltpu.SemaphoreType.DMA((len(inputs),))],
+        compiler_params=pltpu.CompilerParams(vmem_limit_bytes=48 * 2**20),
         name="pack_blocks",
-    )(*inputs)
+    )(blocks, whole)
     groups = [
         [b * group_count + q for b in range(band_count)]
         + [b * group_count + group_count - 1 - q for b in range(band_count)]

time: 28.7 us -> 28.5 us (level); the launches traced: 28.4 us -> 28.5 us
  other arithmetic: 0 us -> 1.65 us
  Pallas kernels: 9.35 us -> 8.02 us
  blocking collectives: 19.1 us -> 18.8 us
    concatenate x0 -> x2, other arithmetic: none -> 1.65 us  [the longest x1 0.88 us: shards(): blocks = jnp.concatenate([visibilities[0], coordinates[0]], axis=1)]
    pallas_call x1, Pallas kernels: 1.99 us -> 0.36 us  [shards(): pl.pallas_call(functools.partial(pack_kernel, band_count, group_count), o...]
    pallas_call x1, Pallas kernels: 7.36 us -> 7.66 us  [shards(): pl.pallas_call(functools.partial(grid_kernel, band_count, group_count), o...]
where the time goes in v3:
time: 28.5 us
  blocking collectives  18.8 us (66%)
  Pallas kernels  8.02 us (28%)
  other arithmetic  1.65 us (6%)
    all_to_all x1, blocking collectives, shards(): lax.all_to_all(message, ('band', 'wgrp'), 0, 0, axis_index_groups=groups,...  18.8 us
    pallas_call x1, Pallas kernels, shards(): pl.pallas_call(functools.partial(grid_kernel, band_count, group_count), o...  7.66 us
    concatenate x1, other arithmetic, shards(): blocks = jnp.concatenate([visibilities[0], coordinates[0]], axis=1)  0.88 us
    concatenate x1, other arithmetic, shards(): whole = jnp.concatenate([block_index, col_offset, counts], axis=1)  0.76 us

profile of v3, /device:TPU:0, one launch (start us, length us, event | category | flops | bytes accessed | tf_op | source)
XLA Modules:
  0.0 28.5 jit_solution(358524637184630584)
XLA Ops:
  0.0 0.9 %pad_maximum_fusion.data_ref = bf16[64,1024]{1,0:T(8,128)(2,1)S(1)} fusion(bf16[64,512]{1,0:T(8,128)(2,1)} %bitcast.7, bf16[64,512]{1,0:T(8,128)(2,1)} %bitcast.8), kind=kLoop, calls=%fused_computation | loop fusion | flops 262144 | bytes 262144 | tf_op jit(solution)/shard_map/concatenate | solution.py:378
  0.9 0.8 %pad_add_fusion.whole_ref = s32[1,136]{1,0:T(1,128)S(1)} fusion(s32[1,8]{1,0:T(1,128)} %param.8, s32[1,64]{1,0:T(1,128)} %param.9, s32[1,64]{1,0:T(1,128)} %param.7), kind=kLoop, calls=%fused_computation.1 | loop fusion | flops 272 | bytes 1088 | tf_op jit(solution)/shard_map/concatenate | solution.py:379
  1.6 0.4 %pack_blocks.1 = bf16[16,8,1152]{2,1,0:T(8,128)(2,1)S(1)} custom-call(bf16[64,1024]{1,0:T(8,128)(2,1)S(1)} %pad_maximum_fusion.data_ref, s32[1,136]{1,0:T(1,128)S(1)} %pad_add_fusion.whole_ref), custom_call_target="tpu_custom_call" | custom-call | tf_op jit(solution)/shard_map/pack_blocks/pallas_call | solution.py:380
  2.0 18.8 %all_to_all.5.recv_ref = bf16[16,8,1152]{2,1,0:T(8,128)(2,1)S(1)} all-to-all(bf16[16,8,1152]{2,1,0:T(8,128)(2,1)S(1)} %pack_blocks.1), channel_id=1, replica_groups={{0,4,8,12,16,20,24,28,3,7,11,15,19,23,27,31},{1,5,9,13,17,21,25,29,2,6,..., dimensions={0} | all-to-all | bytes 589824 | tf_op jit(solution)/shard_map/all_to_all | solution.py:393
  20.9 7.7 %grid_and_transform.1 = f32[2,2048,128]{2,1,0:T(8,128)} custom-call(bf16[16,8,1152]{2,1,0:T(8,128)(2,1)S(1)} %all_to_all.5.recv_ref), custom_call_target="tpu_custom_call" | custom-call | tf_op jit(solution)/shard_map/grid_and_transform/pallas_call | solution.py:399

commit v4 on v3

--- a/solution.py
+++ b/solution.py
@@ -12,6 +12,7 @@
 G = 8192
 K = 256
 GROUP = 2
+STEP = 9
 CAP = 8
 HALF = S // 2
 N1 = 128
@@ -38,13 +39,22 @@
     )
 
 
-def own_base(band_count, group_count):
-    low = lax.axis_index("wgrp") < group_count // 2
-    return jnp.where(low, 0, band_count), jnp.where(low, band_count, 0)
+def exchange_order(band_count):
+    first = band_count * 5 // 8
+    order = []
+    for i in range(band_count):
+        band = (first + i) % band_count
+        order += [(band, 1), (band_count - 1 - band, 0)]
+    return order
+
+
+def in_low_half(group_count):
+    return lax.axis_index("wgrp") < group_count // 2
 
 
 def pack_kernel(band_count, group_count, data_ref, whole_ref, out_ref):
-    own, mirror = own_base(band_count, group_count)
+    below = in_low_half(group_count)
+    order = exchange_order(band_count)
     slots = band_count * CAP
     block_index = whole_ref[:, :slots]
     offsets = whole_ref[:, slots : 2 * slots]
@@ -80,8 +90,9 @@
     for d in range(band_count):
         rows = slice(d * CAP, (d + 1) * CAP)
         message = jnp.concatenate([vis[rows], coord[rows], meta], axis=1).astype(jnp.bfloat16)
-        out_ref[own + d] = message
-        out_ref[mirror + band_count - 1 - d] = message
+        flipped = band_count - 1 - d
+        out_ref[jnp.where(below, order.index((d, 0)), order.index((d, 1)))] = message
+        out_ref[jnp.where(below, order.index((flipped, 1)), order.index((flipped, 0)))] = message
 
 
 def square(z):
@@ -161,7 +172,7 @@
     offset_sem,
     out_sem,
 ):
-    own, _ = own_base(band_count, group_count)
+    below = in_low_half(group_count)
     band = lax.axis_index("band")
 
     slots = 2 * band_count * CAP
@@ -175,7 +186,11 @@
         wanted = jnp.where(pick_row == i + 3, flipped + at, wanted)
     picked = dot_last((pick_col == wanted).astype(jnp.bfloat16), flat[:, DATA:])
     slot = lax.broadcasted_iota(jnp.int32, (1, slots), 1)
-    mine = (slot >= own * CAP) & (slot < (own + band_count) * CAP)
+    from_low = jnp.zeros((1, slots), jnp.int32)
+    for at, (_, half) in enumerate(exchange_order(band_count)):
+        if half == 0:
+            from_low = jnp.where(slot // CAP == at, 1, from_low)
+    mine = from_low == below.astype(jnp.int32)
     high, low, live = (jnp.where(mine, picked[i : i + 1], picked[i + 3 : i + 4]) for i in range(3))
     offsets = (high * 128.0 + low).astype(jnp.int32)
     offsets = jnp.where(mine, offsets, (G - S) - offsets)
@@ -210,21 +225,21 @@
     to_smem.start()
 
     def clear(step, _):
+        rows = pl.ds(pl.multiple_of(step * 24, 24), 24)
         for block in range(S // 8):
-            grid_ref[block, pl.ds(pl.multiple_of(step * 16, 16), 16), :] = jnp.zeros(
-                (16, 128), jnp.float32
-            )
+            grid_ref[block, rows, :] = jnp.zeros((24, 128), jnp.float32)
         return 0
 
-    lax.fori_loop(0, (N1 + 2) // 2, clear, 0)
+    lax.fori_loop(0, grid_ref.shape[1] // 24, clear, 0)
 
     lane = lax.broadcasted_iota(jnp.int32, (8, 128), 1)
     first_half = lane < N2
     lane_in = lane & (N2 - 1)
+    turn_sign = jnp.where(lax.broadcasted_iota(jnp.int32, (S, 128), 1) < N2, -1.0, 1.0)
     chunks = 2 * K // 128
 
     def add_cells(cells, start, offset):
-        row = pl.multiple_of((offset >> 6) * 8, 8)
+        row = (offset >> 6) * STEP
         shift = offset & (N2 - 1)
         near, far = (shift + 128 - start) & 127, (shift + N2 - start) & 127
         stays = (lane_in >= shift) & (lane_in < shift + S)
@@ -235,7 +250,7 @@
             even = jnp.where(first_half, pltpu.roll(upper, near, 1), pltpu.roll(lower, far, 1))
             odd = jnp.where(first_half, pltpu.roll(upper, far, 1), pltpu.roll(lower, near, 1))
             for part, here, over in ((0, even, odd), (1, odd, even)):
-                for at, piece in ((row, jnp.where(stays, here, 0.0)), (row + 8, jnp.where(wraps, over, 0.0))):
+                for at, piece in ((row, jnp.where(stays, here, 0.0)), (row + STEP, jnp.where(wraps, over, 0.0))):
                     rows = pl.ds(at, 8)
                     grid_ref[part * (HALF // 8) + block, rows, :] += piece
 
@@ -256,7 +271,7 @@
             for tab, z, e_part in ((tab_re, weighted[0], e[0]), (tab_im, weighted[1], e[1])):
                 whole = jnp.concatenate([z, e_part[:, K:]], axis=1)
                 for q in range(chunks):
-                    tab[pl.ds(q * 8 * CAP + at, CAP, stride=8), :] = whole[:, q * 128 : (q + 1) * 128]
+                    tab[pl.ds(q * STEP * CAP + at, CAP, stride=STEP), :] = whole[:, q * 128 : (q + 1) * 128]
         eight_re[...] = e8[0]
         eight_im[...] = e8[1]
 
@@ -267,7 +282,7 @@
             for c in range(first, first + GROUP):
                 base = tuple(
                     jnp.concatenate(
-                        [tab[(q * CAP + c) * 8 : (q * CAP + c + 1) * 8, :] for q in range(chunks)],
+                        [tab[(q * CAP + c) * STEP : (q * CAP + c) * STEP + 8, :] for q in range(chunks)],
                         axis=1,
                     )
                     for tab in (tab_re, tab_im)
@@ -281,9 +296,9 @@
                 order = (down2, down, base, up)
                 re = jnp.concatenate([z[0] for z in order], axis=0).astype(jnp.bfloat16)
                 im = jnp.concatenate([z[1] for z in order], axis=0).astype(jnp.bfloat16)
-                left.append(jnp.concatenate([re[:, K:], im[:, K:]], axis=1))
-                real.append(jnp.concatenate([re[:, :K], -im[:, :K]], axis=1))
-                imag.append(jnp.concatenate([im[:, :K], re[:, :K]], axis=1))
+                left += [re[:, K:], im[:, K:]]
+                real.append(re[:, :K])
+                imag.append(im[:, :K])
             right = []
             for c in range(0, GROUP, 2):
                 right += real[c : c + 2] + imag[c : c + 2]
@@ -293,28 +308,37 @@
 
     def keep(products):
         for c in range(CAP):
-            row, tile = c % GROUP * S, c % GROUP // 2 * 128
-            cells_ref[c * S : (c + 1) * S, :] = products[c // GROUP][row : row + S, tile : tile + 128]
+            row, tile = 2 * (c % GROUP) * S, c % GROUP // 2 * 128
+            cells_ref[2 * c * S : 2 * (c + 1) * S, :] = products[c // GROUP][
+                row : row + 2 * S, tile : tile + 128
+            ]
 
     def add_group(group):
         for c in range(CAP):
-            add_cells(cells_ref[c * S : (c + 1) * S, :], c % 2 * S, offset_smem[0, group * CAP + c])
+            by_cos = cells_ref[2 * c * S : (2 * c + 1) * S, :]
+            by_sin = pltpu.roll(cells_ref[(2 * c + 1) * S : (2 * c + 2) * S, :], N2, 1)
+            add_cells(by_cos + turn_sign * by_sin, c % 2 * S, offset_smem[0, group * CAP + c])
 
     make_tables(0, jnp.int32(0))
     fill_tables(outer_ref, inner_ref, twist_ref)
-    cells_ref[...] = jnp.zeros_like(cells_ref)
+    keep(multiply())
     to_smem.wait()
     first_mirrored, groups = offset_smem[1, 0], offset_smem[2, 0]
 
+    def tables_of(group):
+        group = jnp.minimum(group, groups - 1)
+        make_tables(group, (group >= first_mirrored).astype(jnp.int32))
+
+    tables_of(1)
+
     def turn(group, _):
         products = multiply()
-        add_group(jnp.maximum(group - 1, 0))
+        add_group(group - 1)
         keep(products)
-        later = jnp.minimum(group + 1, groups - 1)
-        make_tables(later, (later >= first_mirrored).astype(jnp.int32))
+        tables_of(group + 1)
         return 0
 
-    lax.fori_loop(0, groups, turn, 0)
+    lax.fori_loop(1, groups, turn, 0)
     add_group(groups - 1)
 
     def out_copy(part, group):
@@ -331,7 +355,7 @@
                 jnp.concatenate(
                     [
                         grid_ref[
-                            part * (HALF // 8) + y // 8, pl.ds(y % 8, N1, stride=8), :
+                            part * (HALF // 8) + y // 8, pl.ds(y % 8, N1, stride=STEP), :
                         ].astype(jnp.bfloat16)
                         for y in lines
                     ],
@@ -386,15 +410,14 @@
         name="pack_blocks",
     )(blocks, whole)
     groups = [
-        [b * group_count + q for b in range(band_count)]
-        + [b * group_count + group_count - 1 - q for b in range(band_count)]
+        [b * group_count + (q if half == 0 else group_count - 1 - q) for b, half in exchange_order(band_count)]
         for q in range(group_count // 2)
     ]
     received = lax.all_to_all(
         message, ("band", "wgrp"), 0, 0, axis_index_groups=groups, tiled=True
     )
     slots = peers * CAP
-    base = pltpu.VMEM((2 * K // 128 * 8 * CAP, 128), jnp.float32)
+    base = pltpu.VMEM((2 * K // 128 * STEP * CAP, 128), jnp.float32)
     step = pltpu.VMEM((CAP, 2 * K), jnp.float32)
     rows = pl.pallas_call(
         functools.partial(grid_kernel, band_count, group_count),
@@ -412,8 +435,8 @@
             base,
             step,
             step,
-            pltpu.VMEM((CAP * S, 128), jnp.float32),
-            pltpu.VMEM((S // 8, (N1 + 2) * 8, 128), jnp.float32),
+            pltpu.VMEM((CAP * 2 * S, 128), jnp.float32),
+            pltpu.VMEM((S // 8, pl.cdiv((N1 + 2) * STEP, 24) * 24, 128), jnp.float32),
             pltpu.VMEM((2, S * N2, N1), jnp.float32),
             pltpu.SemaphoreType.DMA(()),
             pltpu.SemaphoreType.DMA((2, S // 8)),

time: 28.5 us -> 24.2 us (0.85)
  the two profiles are of different devices: /device:TPU:0 before, /device:TPU:1 now
where the time goes in v4:
time: 24.2 us; the launch traced here: 24.4 us
  blocking collectives  15.7 us (65%)
  Pallas kernels  7.04 us (29%)
  other arithmetic  1.65 us (7%)
    all_to_all x1, blocking collectives, shards(): lax.all_to_all(message, ('band', 'wgrp'), 0, 0, axis_index_groups=groups,...  15.7 us
    pallas_call x1, Pallas kernels, shards(): pl.pallas_call(functools.partial(grid_kernel, band_count, group_count), o...  6.68 us
    concatenate x1, other arithmetic, shards(): blocks = jnp.concatenate([visibilities[0], coordinates[0]], axis=1)  0.88 us
    concatenate x1, other arithmetic, shards(): whole = jnp.concatenate([block_index, col_offset, counts], axis=1)  0.76 us

profile of v4, /device:TPU:1, one launch (start us, length us, event | category | flops | bytes accessed | tf_op | source)
XLA Modules:
  0.0 24.4 jit_solution(1911826721812989444)
XLA Ops:
  0.0 0.9 %pad_maximum_fusion.data_ref = bf16[64,1024]{1,0:T(8,128)(2,1)S(1)} fusion(bf16[64,512]{1,0:T(8,128)(2,1)} %bitcast.7, bf16[64,512]{1,0:T(8,128)(2,1)} %bitcast.8), kind=kLoop, calls=%fused_computation | loop fusion | flops 262144 | bytes 262144 | tf_op jit(solution)/shard_map/concatenate | solution.py:402
  0.9 0.8 %pad_add_fusion.whole_ref = s32[1,136]{1,0:T(1,128)S(1)} fusion(s32[1,8]{1,0:T(1,128)} %param.8, s32[1,64]{1,0:T(1,128)} %param.9, s32[1,64]{1,0:T(1,128)} %param.7), kind=kLoop, calls=%fused_computation.1 | loop fusion | flops 272 | bytes 1088 | tf_op jit(solution)/shard_map/concatenate | solution.py:403
  1.6 0.4 %pack_blocks.1 = bf16[16,8,1152]{2,1,0:T(8,128)(2,1)S(1)} custom-call(bf16[64,1024]{1,0:T(8,128)(2,1)S(1)} %pad_maximum_fusion.data_ref, s32[1,136]{1,0:T(1,128)S(1)} %pad_add_fusion.whole_ref), custom_call_target="tpu_custom_call" | custom-call | tf_op jit(solution)/shard_map/pack_blocks/pallas_call | solution.py:404
  2.0 15.7 %all_to_all.5.recv_ref = bf16[16,8,1152]{2,1,0:T(8,128)(2,1)S(1)} all-to-all(bf16[16,8,1152]{2,1,0:T(8,128)(2,1)S(1)} %pack_blocks.1), channel_id=1, replica_groups={{23,8,27,4,31,0,3,28,7,24,11,20,15,16,19,12},{22,9,26,5,30,1,2,29,6,25,..., dimensions={0} | all-to-all | bytes 589824 | tf_op jit(solution)/shard_map/all_to_all | solution.py:416
  17.7 6.7 %grid_and_transform.1 = f32[2,2048,128]{2,1,0:T(8,128)} custom-call(bf16[16,8,1152]{2,1,0:T(8,128)(2,1)S(1)} %all_to_all.5.recv_ref), custom_call_target="tpu_custom_call" | custom-call | tf_op jit(solution)/shard_map/grid_and_transform/pallas_call | solution.py:422
